TPU v7x, 128 devices: a whole 4x4x4 slice. The times are simulated.
128 devices in a mesh: head: 4 (over y), ctx: 32 (over x, z, core).
Axes of the slice: x: 4, y: 4, z: 4, core: 2. Of those that a mesh axis runs over, the one named last changes fastest.
Arguments:
- queries: bfloat16 [32, 512, 8192], P('ctx', 'head'), may hold values from -6 to 6
- keys: bfloat16 [32, 512, 8192], P('ctx', 'head'), may hold values from -6 to 6
- values: bfloat16 [32, 512, 8192], P('ctx', 'head'), may hold values from -6 to 6
- gate: bfloat16 [32, 512, 8192], P('ctx', 'head'), may hold values from -6 to 6
- log_decay: float32 [32, 64, 512], P('ctx', 'head'), may hold values from -1 to 0, as said below
- norm_gain: bfloat16 [8192], P('head'), may hold values from 0.099609375 to 1.8984375
Outputs:
- attended: bfloat16 [32, 512, 8192], P('ctx', 'head')
Inputs may be any that keep to these rules, and one draw needn't show every extreme that they name: `log_decay`: every entry is negative.
All inputs are finite; a program needn't handle non-finite values.
Results may differ from a plain program's by a relative error of at most 0.0048.
Values may be sent and summed in bfloat16 or wider, within the bound.
A program may use at most 192 MiB of HBM per device.

v0:
```python
import functools

import jax
import jax.numpy as jnp
from jax import lax
from jax.experimental import pallas as pl
from jax.experimental.pallas import tpu as pltpu
from jax.sharding import PartitionSpec as P

MESH = pl.DeviceIdType.MESH
F32 = jnp.float32
BF16 = jnp.bfloat16
DH = 128
PAD = 8
HIGHEST = lax.Precision.HIGHEST


def at_lanes(head):
    return pl.ds(pl.multiple_of(head * DH, DH), DH)


def kernel(
    dims,
    q_hbm, k_hbm, v_hbm, g_hbm, ld_hbm, gain_hbm,
    o_hbm,
    q, k, v, g, o,
    ld, gain_in, gain,
    cum_row, dec_row, cum_col, step_decay, block_decay,
    s_out, s_in, b_out, b_in, t_out, t_in, c_now, c_out, c_in, p_out, p_in,
    inside, gated,
    load_sem, store_sem,
    ld_send, ld_recv, gain_send, gain_recv,
    s_send, s_recv, b_send, b_recv, t_send, t_recv, c_send, c_recv, p_send, p_recv,
):
    ny, nx, nzc, halves = dims
    rows = q.shape[0]
    per_owner = halves * nzc
    heads = ny * per_owner
    y = lax.axis_index("head")
    ctx = lax.axis_index("ctx")
    x = ctx // nzc
    zc = ctx % nzc

    def load(n, src, dst):
        return pltpu.make_async_copy(src, dst, load_sem.at[n])

    loads = [
        load(0, ld_hbm, ld.at[y]),
        load(1, gain_hbm, gain_in.at[y]),
        load(2, k_hbm, k),
        load(3, v_hbm, v),
        load(4, q_hbm, q),
        load(5, g_hbm, g),
    ]
    for one in loads:
        one.start()

    barrier = pltpu.get_barrier_semaphore()
    peers = [{"head": lax.rem(y + d, ny)} for d in range(1, ny)]
    peers += [{"ctx": x * nzc + lax.rem(zc + e, nzc)} for e in range(1, nzc)]
    peers += [{"ctx": lax.rem(x + d, nx) * nzc + zc} for d in range(1, nx)]
    for peer in peers:
        pl.semaphore_signal(barrier, inc=1, device_id=peer, device_id_type=MESH)
    pl.semaphore_wait(barrier, len(peers))

    def remote(src, dst, send, recv, peer):
        return pltpu.make_async_remote_copy(
            src_ref=src, dst_ref=dst, send_sem=send, recv_sem=recv,
            device_id=peer, device_id_type=MESH,
        )

    def ld_copy(d, source):
        peer = {"head": lax.rem(y + d, ny)}
        return remote(ld.at[source], ld.at[source], ld_send.at[d - 1], ld_recv.at[d - 1], peer)

    def gain_copy(d, source):
        peer = {"head": lax.rem(y + d, ny)}
        return remote(
            gain_in.at[source], gain_in.at[source], gain_send.at[d - 1], gain_recv.at[d - 1], peer
        )

    loads[0].wait()
    for d in range(1, ny):
        ld_copy(d, y).start()
    loads[1].wait()
    for d in range(1, ny):
        gain_copy(d, y).start()
    for d in range(1, ny):
        ld_copy(d, lax.rem(y + ny - d, ny)).wait_recv()

    upper = (
        lax.broadcasted_iota(jnp.int32, (rows, rows), 0)
        <= lax.broadcasted_iota(jnp.int32, (rows, rows), 1)
    ).astype(F32)
    mine = pl.ds(pl.multiple_of(y * rows, rows), rows)
    cum_col[...] = jnp.zeros_like(cum_col)
    for group in range(ny):
        cumulative = jnp.dot(
            ld[group, :, mine], upper, precision=HIGHEST, preferred_element_type=F32
        )
        here = pl.ds(group * per_owner, per_owner)
        cum_row[here, :] = cumulative
        dec_row[here, :] = jnp.exp(cumulative[:, rows - 1 :] - cumulative)
        cum_col[here, :] = cumulative
    cum_col[...] = cum_col[...].T
    whole = jnp.zeros((per_owner, 1), F32)
    for part in range(ny):
        total = jnp.sum(ld[y, :, part * rows : (part + 1) * rows], axis=1, keepdims=True)
        step_decay[part] = jnp.broadcast_to(jnp.exp(total), (per_owner, DH))
        whole = whole + total
    block_decay[...] = jnp.broadcast_to(jnp.exp(whole), (per_owner, DH))

    def s_copy(half, d, source, peer_group):
        here = pl.ds(peer_group * per_owner + half * nzc, nzc)
        there = pl.ds(half * nzc, nzc)
        return remote(
            s_out.at[here], s_in.at[source, there], s_send.at[half, d - 1], s_recv.at[half, d - 1],
            {"head": lax.rem(y + d, ny)},
        )

    def state_of(head):
        lanes = at_lanes(head)
        decayed = (k[:, lanes].astype(F32).T * dec_row[pl.ds(head, 1), :]).astype(BF16)
        return jnp.dot(decayed, v[:, lanes], preferred_element_type=F32).astype(BF16)

    order = [d for d in (2, 1, 3) if d < ny]
    loads[2].wait()
    loads[3].wait()
    for half in range(halves):
        for d in order + [0]:
            group = lax.rem(y + d, ny)

            def one_state(j, _, group=group, half=half, d=d):
                local = half * nzc + j
                state = state_of(group * per_owner + local)
                if d == 0:
                    s_in[y, local] = state
                else:
                    s_out[group * per_owner + local] = state
                return 0

            lax.fori_loop(0, nzc, one_state, 0)
            if d:
                s_copy(half, d, y, group).start()

    loads[4].wait()
    loads[5].wait()
    for d in range(1, ny):
        gain_copy(d, lax.rem(y + ny - d, ny)).wait_recv()
    for group in range(ny):
        gain[pl.ds(group * per_owner, per_owner), :] = gain_in[group].astype(F32)

    causal = lax.broadcasted_iota(jnp.int32, (rows, rows), 0) >= lax.broadcasted_iota(
        jnp.int32, (rows, rows), 1
    )

    def column_of(head):
        turned = pltpu.roll(cum_col[...], lax.rem(DH - head, DH), axis=1)
        return jnp.broadcast_to(turned[:, :1], (rows, rows))

    def one_inside(head, _):
        lanes = at_lanes(head)
        scores = lax.dot_general(
            q[:, lanes], k[:, lanes], (((1,), (1,)), ((), ())), preferred_element_type=F32
        )
        gap = jnp.where(causal, column_of(head) - cum_row[pl.ds(head, 1), :], -jnp.inf)
        weights = (scores * jnp.exp(gap)).astype(BF16)
        inside[:, lanes] = jnp.dot(weights, v[:, lanes], preferred_element_type=F32)
        gated[:, lanes] = jax.nn.sigmoid(g[:, lanes].astype(F32)) * gain[pl.ds(head, 1), :]
        return 0

    def b_copy(half, e, source, owner):
        return remote(
            b_out.at[half, owner], b_in.at[half, source], b_send.at[half, e - 1],
            b_recv.at[half, e - 1], {"ctx": x * nzc + owner},
        )

    def t_copy(half, d):
        return remote(
            t_out.at[half], t_in.at[half, d - 1], t_send.at[half, d - 1], t_recv.at[half, d - 1],
            {"ctx": lax.rem(x + d, nx) * nzc + zc},
        )

    def c_copy(half, e, source, block):
        return remote(
            c_out.at[half, block], c_in.at[half, source], c_send.at[half, e - 1],
            c_recv.at[half, e - 1], {"ctx": x * nzc + block},
        )

    def p_copy(half, d, source, part):
        there = pl.ds(half * nzc, nzc)
        return remote(
            p_out.at[part, there], p_in.at[source, there], p_send.at[half, d - 1],
            p_recv.at[half, d - 1], {"head": part},
        )

    def make_totals(half):
        for d in range(1, ny):
            s_copy(half, d, lax.rem(y + ny - d, ny), lax.rem(y + d, ny)).wait_recv()

        def one_total(r, _):
            local = half * nzc + r
            total = s_in[0, local].astype(F32)
            for part in range(1, ny):
                total = total * step_decay[part, pl.ds(local, 1), :] + s_in[part, local].astype(F32)
            b_out[half, r, :DH, :] = total
            b_out[half, r, DH:, :] = jnp.broadcast_to(block_decay[pl.ds(local, 1), :], (PAD, DH))
            return 0

        lax.fori_loop(0, nzc, one_total, 0)
        for e in range(1, nzc):
            b_copy(half, e, zc, lax.rem(zc + e, nzc)).start()
        b_in[half, zc] = b_out[half, zc]

    def make_group_total(half):
        for e in range(1, nzc):
            b_copy(half, e, lax.rem(zc + nzc - e, nzc), lax.rem(zc + e, nzc)).wait_recv()
        total = b_in[half, 0, :DH, :]
        decay = b_in[half, 0, DH:, :]
        for block in range(1, nzc):
            step = b_in[half, block, DH:, :]
            total = total * step[:1] + b_in[half, block, :DH, :]
            decay = decay * step
        t_out[half, :DH, :] = total
        t_out[half, DH:, :] = decay
        for d in range(1, nx):

            @pl.when(x + d < nx)
            def _(d=d):
                t_copy(half, d).start()

    def make_carried(half):
        c_now[...] = jnp.zeros_like(c_now)
        for d in range(nx - 1, 0, -1):

            @pl.when(x >= d)
            def _(d=d):
                t_copy(half, d).wait_recv()
                c_now[...] = c_now[...] * t_in[half, d - 1, DH : DH + 1, :] + t_in[half, d - 1, :DH, :]

        state = c_now[...]
        for block in range(nzc):
            c_out[half, block] = state
            if block + 1 < nzc:
                state = state * b_in[half, block, DH : DH + 1, :] + b_in[half, block, :DH, :]
        for e in range(1, nzc):
            c_copy(half, e, zc, lax.rem(zc + e, nzc)).start()
        c_in[half, zc] = c_out[half, zc]

    def make_prefixes(half):
        for e in range(1, nzc):
            c_copy(half, e, lax.rem(zc + nzc - e, nzc), lax.rem(zc + e, nzc)).wait_recv()

        def one_prefix(r, _):
            local = half * nzc + r
            state = c_in[half, r]
            for part in range(ny):
                p_out[part, local] = state.astype(BF16)
                if part + 1 < ny:
                    decay = step_decay[part, pl.ds(local, 1), :]
                    state = state * decay + s_in[part, local].astype(F32)
            return 0

        lax.fori_loop(0, nzc, one_prefix, 0)
        for d in order:
            p_copy(half, d, y, lax.rem(y + d, ny)).start()
        there = pl.ds(half * nzc, nzc)
        p_in[y, there] = p_out[y, there]

    def store(half, group, d):
        lanes = pl.ds(pl.multiple_of((group * per_owner + half * nzc) * DH, DH), nzc * DH)
        return pltpu.make_async_copy(o.at[:, lanes], o_hbm.at[:, lanes], store_sem.at[half, d])

    def make_outputs(half, d):
        group = lax.rem(y + ny - d, ny)
        if d:
            p_copy(half, d, group, lax.rem(y + d, ny)).wait_recv()

        def one_output(j, _):
            local = half * nzc + j
            head = group * per_owner + local
            lanes = at_lanes(head)
            from_state = jnp.dot(q[:, lanes], p_in[group, local], preferred_element_type=F32)
            mixed = inside[:, lanes] + jnp.exp(column_of(head)) * from_state
            scale = lax.rsqrt(jnp.mean(mixed * mixed, axis=1, keepdims=True) + 1e-6)
            o[:, lanes] = (mixed * scale * gated[:, lanes]).astype(BF16)
            return 0

        lax.fori_loop(0, nzc, one_output, 0)
        store(half, group, d).start()

    quarter = heads // 4
    lax.fori_loop(0, quarter, one_inside, 0)
    make_totals(0)
    lax.fori_loop(quarter, 2 * quarter, one_inside, 0)
    make_group_total(0)
    lax.fori_loop(2 * quarter, 3 * quarter, one_inside, 0)
    make_carried(0)
    make_totals(1)
    lax.fori_loop(3 * quarter, heads, one_inside, 0)
    make_prefixes(0)
    make_group_total(1)
    make_outputs(0, 0)
    make_carried(1)
    for d in order[:1]:
        make_outputs(0, d)
    make_prefixes(1)
    for d in order[1:]:
        make_outputs(0, d)
    make_outputs(1, 0)
    for d in order:
        make_outputs(1, d)

    for d in range(1, ny):
        ld_copy(d, y).wait_send()
        gain_copy(d, y).wait_send()
    for half in range(halves):
        for d in range(1, ny):
            s_copy(half, d, y, lax.rem(y + d, ny)).wait_send()
            p_copy(half, d, y, lax.rem(y + d, ny)).wait_send()
        for e in range(1, nzc):
            b_copy(half, e, zc, lax.rem(zc + e, nzc)).wait_send()
            c_copy(half, e, zc, lax.rem(zc + e, nzc)).wait_send()
        for d in range(1, nx):

            @pl.when(x + d < nx)
            def _(half=half, d=d):
                t_copy(half, d).wait_send()

        for d in range(ny):
            store(half, lax.rem(y + ny - d, ny), d).wait()


def on_device(dims, queries, keys, values, gate, log_decay, norm_gain):
    ny, nx, nzc, halves = dims
    per_owner = halves * nzc
    heads = ny * per_owner
    _, rows, width = queries.shape
    block = log_decay.shape[2]
    dma = pltpu.SemaphoreType.DMA
    vmem = pltpu.VMEM
    stream = [vmem((rows, width), BF16)] * 5
    out = pl.pallas_call(
        functools.partial(kernel, dims),
        out_shape=jax.ShapeDtypeStruct((rows, width), BF16),
        in_specs=[pl.BlockSpec(memory_space=pl.ANY)] * 6,
        out_specs=pl.BlockSpec(memory_space=pl.ANY),
        scratch_shapes=stream
        + [
            vmem((ny, per_owner, block), F32),
            vmem((ny, per_owner, DH), BF16),
            vmem((heads, DH), F32),
            vmem((heads, rows), F32),
            vmem((heads, rows), F32),
            vmem((rows, rows), F32),
            vmem((ny, per_owner, DH), F32),
            vmem((per_owner, DH), F32),
            vmem((heads, DH, DH), BF16),
            vmem((ny, per_owner, DH, DH), BF16),
            vmem((halves, nzc, DH + PAD, DH), F32),
            vmem((halves, nzc, DH + PAD, DH), F32),
            vmem((halves, DH + PAD, DH), F32),
            vmem((halves, nx - 1, DH + PAD, DH), F32),
            vmem((DH, DH), F32),
            vmem((halves, nzc, DH, DH), F32),
            vmem((halves, nzc, DH, DH), F32),
            vmem((ny, per_owner, DH, DH), BF16),
            vmem((ny, per_owner, DH, DH), BF16),
            vmem((rows, width), F32),
            vmem((rows, width), F32),
            dma((6,)),
            dma((halves, ny)),
            dma((ny - 1,)),
            dma((ny - 1,)),
            dma((ny - 1,)),
            dma((ny - 1,)),
            dma((halves, ny - 1)),
            dma((halves, ny - 1)),
            dma((halves, nzc - 1)),
            dma((halves, nzc - 1)),
            dma((halves, nx - 1)),
            dma((halves, nx - 1)),
            dma((halves, nzc - 1)),
            dma((halves, nzc - 1)),
            dma((halves, ny - 1)),
            dma((halves, ny - 1)),
        ],
        compiler_params=pltpu.CompilerParams(
            collective_id=0, has_side_effects=True, vmem_limit_bytes=52 * 2**20
        ),
        cost_estimate=pl.CostEstimate(
            flops=8 * rows * DH * width, bytes_accessed=10 * rows * width, transcendentals=0
        ),
    )(
        queries[0],
        keys[0],
        values[0],
        gate[0],
        log_decay[0],
        norm_gain.reshape(per_owner, DH),
    )
    return out[None]


def solution(mesh):
    ny = mesh.shape["head"]
    nctx = mesh.shape["ctx"]
    nx = 4 if nctx >= 16 else 2
    halves = 2

    def whole(queries, keys, values, gate, log_decay, norm_gain):
        dims = (ny, nx, nctx // nx, halves)
        return jax.shard_map(
            functools.partial(on_device, dims),
            mesh=mesh,
            in_specs=(P("ctx", "head", None),) * 5 + (P("head"),),
            out_specs=P("ctx", "head", None),
            check_vma=False,
        )(queries, keys, values, gate, log_decay, norm_gain)

    return whole
```

profile of v0, /device:TPU:7, one launch (start us, length us, event | category | flops | bytes accessed | tf_op | source)
XLA Modules:
  0.0 92.3 jit_solution(15498662892543291793)
XLA Ops:
  0.0 0.0 copy-start
  0.0 0.8 copy-done
  0.8 0.0 copy-start.1
  0.8 0.7 copy-done.1
  1.4 87.8 %shard_map.64 = bf16[128,8192]{1,0:T(8,128)(2,1)} custom-call(bf16[128,8192]{1,0:T(8,128)(2,1)} %bitcast.10, bf16[128,8192]{1,0:T(8,128)(2,1)} %bitcast.11, bf16[128,8192]{1,0:T(8,128)(2,1)} %bitcast.12, bf16[128,8192]{1,0:T(8,128)(2,1)} %bitcast.13, f32[16,512]{1,0:T(8,128)S(1)} %bitcast.7, bf16[16,128]{1,0:T(8,128)(2,1)S(1)} %bitcast.8), custom_call_target="tpu_custom_call" | custom-call | flops 1073741824 | bytes 10485760 | tf_op jit(solution)/shard_map/pallas_call | solution.py:343
  89.2 3.1 %copy.8 = bf16[1,128,8192]{2,1,0:T(8,128)(2,1)} copy(bf16[1,128,8192]{2,1,0:T(8,128)(2,1)} %bitcast.9) | data formatting | bytes 4194304
Async XLA Ops:
  0.0 0.8 copy-start
  0.8 0.7 copy-start.1
where the time goes:
time: 92.5 us; the launch traced here: 92.3 us
  Pallas kernels  87.8 us (95%)
  local copies, waits for them, and re-layouts  4.54 us (5%)
    pallas_call x1, Pallas kernels, on_device(): pl.pallas_call(functools.partial(kernel, dims), out_shape=jax.ShapeDtypeS...  87.8 us
    unnamed x5, local copies, waits for them, and re-layouts  4.54 us

commit v1 on v0

v1 whole, which is shorter than its diff:
```python
import functools

import jax
import jax.numpy as jnp
from jax import lax
from jax.experimental import pallas as pl
from jax.experimental.pallas import tpu as pltpu
from jax.sharding import PartitionSpec as P

MESH = pl.DeviceIdType.MESH
F32 = jnp.float32
BF16 = jnp.bfloat16
DH = 128
PAD = 8
HIGHEST = lax.Precision.HIGHEST


def kernel(
    dims,
    q_hbm, k_hbm, v_hbm, g_hbm, ld_hbm, gain_hbm,
    o_hbm,
    q, k, v, g, o,
    ld, gain_in, gain,
    cum_row, dec_row, cum_col, exp_col, step_decay, block_decay,
    s_out, s_in, b_out, b_in, t_out, t_in, c_now, c_out, c_in, p_out, p_in,
    inside, gated,
    load_sem, store_sem,
    ld_send, ld_recv, gain_send, gain_recv,
    s_send, s_recv, b_send, b_recv, t_send, t_recv, c_send, c_recv, p_send, p_recv,
):
    ny, nx, nzc, chunks, few = dims
    rows = q.shape[0]
    per_owner = chunks * few
    heads = ny * per_owner
    pieces = nzc // few
    piece = DH // pieces
    y = lax.axis_index("head")
    ctx = lax.axis_index("ctx")
    x = ctx // nzc
    zc = ctx % nzc

    def load(n, src, dst):
        return pltpu.make_async_copy(src, dst, load_sem.at[n])

    loads = [
        load(0, ld_hbm, ld.at[y]),
        load(1, gain_hbm, gain_in.at[y]),
        load(2, k_hbm, k),
        load(3, v_hbm, v),
        load(4, q_hbm, q),
        load(5, g_hbm, g),
    ]
    for one in loads:
        one.start()

    barrier = pltpu.get_barrier_semaphore()
    peers = [{"head": lax.rem(y + d, ny)} for d in range(1, ny)]
    peers += [{"ctx": x * nzc + lax.rem(zc + e, nzc)} for e in range(1, nzc)]
    peers += [{"ctx": lax.rem(x + d, nx) * nzc + zc} for d in range(1, nx)]
    for peer in peers:
        pl.semaphore_signal(barrier, inc=1, device_id=peer, device_id_type=MESH)
    pl.semaphore_wait(barrier, len(peers))

    def remote(src, dst, send, recv, peer):
        return pltpu.make_async_remote_copy(
            src_ref=src, dst_ref=dst, send_sem=send, recv_sem=recv,
            device_id=peer, device_id_type=MESH,
        )

    def ld_copy(d, source):
        peer = {"head": lax.rem(y + d, ny)}
        return remote(ld.at[source], ld.at[source], ld_send.at[d - 1], ld_recv.at[d - 1], peer)

    def gain_copy(d, source):
        peer = {"head": lax.rem(y + d, ny)}
        return remote(
            gain_in.at[source], gain_in.at[source], gain_send.at[d - 1], gain_recv.at[d - 1], peer
        )

    loads[0].wait()
    for d in range(1, ny):
        ld_copy(d, y).start()
    loads[1].wait()
    for d in range(1, ny):
        gain_copy(d, y).start()
    for d in range(1, ny):
        ld_copy(d, lax.rem(y + ny - d, ny)).wait_recv()

    upper = (
        lax.broadcasted_iota(jnp.int32, (rows, rows), 0)
        <= lax.broadcasted_iota(jnp.int32, (rows, rows), 1)
    ).astype(F32)
    mine = pl.ds(pl.multiple_of(y * rows, rows), rows)
    cum_col[...] = jnp.zeros_like(cum_col)
    for group in range(ny):
        cumulative = jnp.dot(
            ld[group, :, mine], upper, precision=HIGHEST, preferred_element_type=F32
        )
        here = pl.ds(group * per_owner, per_owner)
        cum_row[here, :] = cumulative
        dec_row[here, :] = jnp.exp(cumulative[:, rows - 1 :] - cumulative)
        cum_col[here, :] = cumulative
    cum_col[...] = cum_col[...].T
    exp_col[...] = jnp.exp(cum_col[...])
    whole = jnp.zeros((per_owner, 1), F32)
    for part in range(ny):
        total = jnp.sum(ld[y, :, part * rows : (part + 1) * rows], axis=1, keepdims=True)
        step_decay[part] = jnp.broadcast_to(jnp.exp(total), (per_owner, DH))
        whole = whole + total
    block_decay[...] = jnp.broadcast_to(jnp.exp(whole), (per_owner, DH))

    def s_copy(i, d, source, group):
        here = pl.ds(group * per_owner + i * few, few)
        there = pl.ds(i * few, few)
        return remote(
            s_out.at[here], s_in.at[source, there], s_send.at[i, d - 1], s_recv.at[i, d - 1],
            {"head": lax.rem(y + d, ny)},
        )

    def b_copy(i, e, source, owner):
        return remote(
            b_out.at[i, owner], b_in.at[i, source], b_send.at[i, e - 1], b_recv.at[i, e - 1],
            {"ctx": x * nzc + owner},
        )

    def t_copy(i, d):
        return remote(
            t_out.at[i], t_in.at[i, d - 1], t_send.at[i, d - 1], t_recv.at[i, d - 1],
            {"ctx": lax.rem(x + d, nx) * nzc + zc},
        )

    def c_copy(i, e, source, block):
        return remote(
            c_out.at[i, block], c_in.at[i, source], c_send.at[i, e - 1], c_recv.at[i, e - 1],
            {"ctx": x * nzc + block},
        )

    def p_copy(i, d, source, part):
        there = pl.ds(i * few, few)
        return remote(
            p_out.at[part, there], p_in.at[source, there], p_send.at[i, d - 1], p_recv.at[i, d - 1],
            {"head": part},
        )

    def store(i, d):
        group = lax.rem(y + ny - d, ny)
        lanes = pl.ds(pl.multiple_of((group * per_owner + i * few) * DH, DH), few * DH)
        return pltpu.make_async_copy(o.at[:, lanes], o_hbm.at[:, lanes], store_sem.at[i, d])

    def lanes_of(first, j):
        return pl.ds(pl.multiple_of((first + j) * DH, DH), DH)

    far_first = [d for d in (2, 1, 3) if d < ny]

    def make_states(i):
        for d in far_first + [0]:
            group = lax.rem(y + d, ny)
            begin = pl.multiple_of(group * per_owner, per_owner)
            for j in range(i * few, (i + 1) * few):
                lanes = lanes_of(begin, j)
                decay = dec_row[pl.ds(begin, per_owner), :][j : j + 1]
                decayed = (k[:, lanes].T.astype(F32) * decay).astype(BF16)
                state = jnp.dot(decayed, v[:, lanes], preferred_element_type=F32).astype(BF16)
                if d:
                    s_out[begin + j] = state
                else:
                    s_in[y, j] = state

    def send_states(i):
        for d in far_first:
            s_copy(i, d, y, lax.rem(y + d, ny)).start()

    causal = lax.broadcasted_iota(jnp.int32, (rows, rows), 0) >= lax.broadcasted_iota(
        jnp.int32, (rows, rows), 1
    )
    wide = 8 if heads % 8 == 0 else heads

    def make_inside(step):
        first = pl.multiple_of(step * wide, wide)
        columns = pltpu.roll(cum_col[...], lax.rem(DH - first, DH), axis=1)[:, :wide]
        sums = cum_row[pl.ds(first, wide), :]
        gains = gain[pl.ds(first, wide), :]
        for j in range(wide):
            lanes = lanes_of(first, j)
            scores = lax.dot_general(
                q[:, lanes], k[:, lanes], (((1,), (1,)), ((), ())), preferred_element_type=F32
            )
            gap = jnp.where(causal, columns[:, j : j + 1] - sums[j : j + 1], -jnp.inf)
            weights = (scores * jnp.exp(gap)).astype(BF16)
            inside[:, lanes] = jnp.dot(weights, v[:, lanes], preferred_element_type=F32)
            gated[:, lanes] = jax.nn.sigmoid(g[:, lanes].astype(F32)) * gains[j : j + 1]

    def many_inside(start, stop):
        def one(step, _):
            make_inside(step)
            return 0

        lax.fori_loop(start, stop, one, 0)

    def await_states(i):
        for d in range(1, ny):
            s_copy(i, d, lax.rem(y + ny - d, ny), lax.rem(y + d, ny)).wait_recv()

    def make_totals(i):
        for j in range(few):
            local = i * few + j
            total = s_in[0, local].astype(F32)
            for part in range(1, ny):
                total = total * step_decay[part, local : local + 1, :] + s_in[part, local].astype(F32)
            for n in range(pieces):
                b_out[i, j * pieces + n, :piece, :] = total[n * piece : (n + 1) * piece]
                b_out[i, j * pieces + n, piece:, :] = jnp.broadcast_to(
                    block_decay[local : local + 1, :], (PAD, DH)
                )
        for e in range(1, nzc):
            b_copy(i, e, zc, lax.rem(zc + e, nzc)).start()
        b_in[i, zc] = b_out[i, zc]

    def make_group_total(i):
        for e in range(1, nzc):
            b_copy(i, e, lax.rem(zc + nzc - e, nzc), lax.rem(zc + e, nzc)).wait_recv()
        total = b_in[i, 0, :piece, :]
        decay = b_in[i, 0, piece:, :]
        for block in range(1, nzc):
            step = b_in[i, block, piece:, :]
            total = total * step[:1] + b_in[i, block, :piece, :]
            decay = decay * step
        t_out[i, :piece, :] = total
        t_out[i, piece:, :] = decay
        for d in range(1, nx):

            @pl.when(x + d < nx)
            def _(d=d):
                t_copy(i, d).start()

    def make_carried(i):
        c_now[...] = jnp.zeros_like(c_now)
        for d in range(nx - 1, 0, -1):

            @pl.when(x >= d)
            def _(d=d):
                t_copy(i, d).wait_recv()
                c_now[...] = c_now[...] * t_in[i, d - 1, piece : piece + 1, :] + t_in[i, d - 1, :piece, :]

        state = c_now[...]
        for block in range(nzc):
            c_out[i, block] = state
            if block + 1 < nzc:
                state = state * b_in[i, block, piece : piece + 1, :] + b_in[i, block, :piece, :]
        for e in range(1, nzc):
            c_copy(i, e, zc, lax.rem(zc + e, nzc)).start()
        c_in[i, zc] = c_out[i, zc]

    def make_prefixes(i):
        for e in range(1, nzc):
            c_copy(i, e, lax.rem(zc + nzc - e, nzc), lax.rem(zc + e, nzc)).wait_recv()
        for j in range(few):
            local = i * few + j
            state = c_in[i, j * pieces : (j + 1) * pieces].reshape(DH, DH)
            for part in range(ny):
                p_out[part, local] = state.astype(BF16)
                if part + 1 < ny:
                    decay = step_decay[part, local : local + 1, :]
                    state = state * decay + s_in[part, local].astype(F32)
        for d in far_first:
            p_copy(i, d, y, lax.rem(y + d, ny)).start()
        there = pl.ds(i * few, few)
        p_in[y, there] = p_out[y, there]

    def make_outputs(i, d):
        group = lax.rem(y + ny - d, ny)
        if d:
            p_copy(i, d, group, lax.rem(y + d, ny)).wait_recv()
        begin = pl.multiple_of(group * per_owner, per_owner)
        first = begin + i * few
        columns = pltpu.roll(exp_col[...], lax.rem(DH - first, DH), axis=1)[:, :few]
        for j in range(few):
            lanes = lanes_of(first, j)
            from_state = jnp.dot(
                q[:, lanes], p_in[group, i * few + j], preferred_element_type=F32
            )
            mixed = inside[:, lanes] + columns[:, j : j + 1] * from_state
            scale = lax.rsqrt(jnp.mean(mixed * mixed, axis=1, keepdims=True) + 1e-6)
            o[:, lanes] = (mixed * scale * gated[:, lanes]).astype(BF16)
        store(i, d).start()

    def ready_rest():
        loads[4].wait()
        loads[5].wait()
        for d in range(1, ny):
            gain_copy(d, lax.rem(y + ny - d, ny)).wait_recv()
        for group in range(ny):
            gain[pl.ds(group * per_owner, per_owner), :] = gain_in[group].astype(F32)

    steps = heads // wide
    eighth = [steps * n // 8 for n in range(9)]

    def ins(n):
        many_inside(eighth[n], eighth[n + 1])

    loads[2].wait()
    loads[3].wait()
    make_states(0)
    send_states(0)
    make_states(1)
    ready_rest()
    ins(0)
    send_states(1)
    make_states(2)
    make_states(3)
    ins(1)
    await_states(0)
    send_states(2)
    make_totals(0)
    ins(2)
    await_states(1)
    send_states(3)
    make_totals(1)
    make_group_total(0)
    ins(3)
    make_carried(0)
    ins(4)
    make_group_total(1)
    make_prefixes(0)
    await_states(2)
    make_totals(2)
    make_carried(1)
    ins(5)
    make_group_total(2)
    make_prefixes(1)
    await_states(3)
    make_totals(3)
    make_carried(2)
    ins(6)
    make_group_total(3)
    make_prefixes(2)
    ins(7)
    make_carried(3)
    for d in [0] + far_first:
        make_outputs(0, d)
    make_prefixes(3)
    for i in range(1, chunks):
        for d in [0] + far_first:
            make_outputs(i, d)

    for d in range(1, ny):
        ld_copy(d, y).wait_send()
        gain_copy(d, y).wait_send()
    for i in range(chunks):
        for d in range(1, ny):
            s_copy(i, d, y, lax.rem(y + d, ny)).wait_send()
            p_copy(i, d, y, lax.rem(y + d, ny)).wait_send()
        for e in range(1, nzc):
            b_copy(i, e, zc, lax.rem(zc + e, nzc)).wait_send()
            c_copy(i, e, zc, lax.rem(zc + e, nzc)).wait_send()
        for d in range(1, nx):

            @pl.when(x + d < nx)
            def _(i=i, d=d):
                t_copy(i, d).wait_send()

        for d in range(ny):
            store(i, d).wait()


def on_device(dims, queries, keys, values, gate, log_decay, norm_gain):
    ny, nx, nzc, chunks, few = dims
    per_owner = chunks * few
    pieces = nzc // few
    piece = DH // pieces
    heads = ny * per_owner
    _, rows, width = queries.shape
    block = log_decay.shape[2]
    dma = pltpu.SemaphoreType.DMA
    vmem = pltpu.VMEM
    stream = [vmem((rows, width), BF16)] * 5
    out = pl.pallas_call(
        functools.partial(kernel, dims),
        out_shape=jax.ShapeDtypeStruct((rows, width), BF16),
        in_specs=[pl.BlockSpec(memory_space=pl.ANY)] * 6,
        out_specs=pl.BlockSpec(memory_space=pl.ANY),
        scratch_shapes=stream
        + [
            vmem((ny, per_owner, block), F32),
            vmem((ny, per_owner, DH), BF16),
            vmem((heads, DH), F32),
            vmem((heads, rows), F32),
            vmem((heads, rows), F32),
            vmem((rows, rows), F32),
            vmem((rows, rows), F32),
            vmem((ny, per_owner, DH), F32),
            vmem((per_owner, DH), F32),
            vmem((heads, DH, DH), BF16),
            vmem((ny, per_owner, DH, DH), BF16),
            vmem((chunks, nzc, piece + PAD, DH), F32),
            vmem((chunks, nzc, piece + PAD, DH), F32),
            vmem((chunks, piece + PAD, DH), F32),
            vmem((chunks, nx - 1, piece + PAD, DH), F32),
            vmem((piece, DH), F32),
            vmem((chunks, nzc, piece, DH), F32),
            vmem((chunks, nzc, piece, DH), F32),
            vmem((ny, per_owner, DH, DH), BF16),
            vmem((ny, per_owner, DH, DH), BF16),
            vmem((rows, width), F32),
            vmem((rows, width), F32),
            dma((6,)),
            dma((chunks, ny)),
            dma((ny - 1,)),
            dma((ny - 1,)),
            dma((ny - 1,)),
            dma((ny - 1,)),
            dma((chunks, ny - 1)),
            dma((chunks, ny - 1)),
            dma((chunks, nzc - 1)),
            dma((chunks, nzc - 1)),
            dma((chunks, nx - 1)),
            dma((chunks, nx - 1)),
            dma((chunks, nzc - 1)),
            dma((chunks, nzc - 1)),
            dma((chunks, ny - 1)),
            dma((chunks, ny - 1)),
        ],
        compiler_params=pltpu.CompilerParams(
            collective_id=0, has_side_effects=True, vmem_limit_bytes=52 * 2**20
        ),
        cost_estimate=pl.CostEstimate(
            flops=8 * rows * DH * width, bytes_accessed=10 * rows * width, transcendentals=0
        ),
    )(
        queries[0],
        keys[0],
        values[0],
        gate[0],
        log_decay[0],
        norm_gain.reshape(per_owner, DH),
    )
    return out[None]


def solution(mesh):
    ny = mesh.shape["head"]
    nctx = mesh.shape["ctx"]
    nx = 4 if nctx >= 16 else 2
    def whole(queries, keys, values, gate, log_decay, norm_gain):
        chunks = 4
        few = log_decay.shape[1] // (ny * chunks)
        dims = (ny, nx, nctx // nx, chunks, few)
        return jax.shard_map(
            functools.partial(on_device, dims),
            mesh=mesh,
            in_specs=(P("ctx", "head", None),) * 5 + (P("head"),),
            out_specs=P("ctx", "head", None),
            check_vma=False,
        )(queries, keys, values, gate, log_decay, norm_gain)

    return whole
```

time: 92.5 us -> 75 us (0.81)
  Pallas kernels: 87.8 us -> 70 us
    pallas_call x1, Pallas kernels: 87.8 us -> 70 us  [on_device(): pl.pallas_call(functools.partial(kernel, dims), out_shape=jax.ShapeDtypeS...]
where the time goes in v1:
time: 75 us; the launch traced here: 74.5 us
  Pallas kernels  70 us (93%)
  local copies, waits for them, and re-layouts  4.54 us (6%)
    pallas_call x1, Pallas kernels, on_device(): pl.pallas_call(functools.partial(kernel, dims), out_shape=jax.ShapeDtypeS...  70 us
    unnamed x5, local copies, waits for them, and re-layouts  4.54 us

profile of v1, /device:TPU:7, one launch (start us, length us, event | category | flops | bytes accessed | tf_op | source)
XLA Modules:
  0.0 74.5 jit_solution(12033913522227051609)
XLA Ops:
  0.0 0.0 copy-start
  0.0 0.8 %copy-done = f32[1,16,512]{2,1,0:T(8,128)S(1)} copy-done((f32[1,16,512]{2,1,0:T(8,128)S(1)}, f32[1,16,512]{2,1,0:T(8,128)}, u32[]{:S(2)}) %copy-start) | copy-done | bytes 32792
  0.8 0.0 copy-start.1
  0.8 0.7 copy-done.1
  1.4 70.0 %shard_map.64 = bf16[128,8192]{1,0:T(8,128)(2,1)} custom-call(bf16[128,8192]{1,0:T(8,128)(2,1)} %bitcast.10, bf16[128,8192]{1,0:T(8,128)(2,1)} %bitcast.11, bf16[128,8192]{1,0:T(8,128)(2,1)} %bitcast.12, bf16[128,8192]{1,0:T(8,128)(2,1)} %bitcast.13, f32[16,512]{1,0:T(8,128)S(1)} %bitcast.7, bf16[16,128]{1,0:T(8,128)(2,1)S(1)} %bitcast.8), custom_call_target="tpu_custom_call" | custom-call | flops 1073741824 | bytes 10485760 | tf_op jit(solution)/shard_map/pallas_call | solution.py:377
  71.4 3.1 %copy.8 = bf16[1,128,8192]{2,1,0:T(8,128)(2,1)} copy(bf16[1,128,8192]{2,1,0:T(8,128)(2,1)} %bitcast.9) | data formatting | bytes 4194304
Async XLA Ops:
  0.0 0.8 %copy-start = (f32[1,16,512]{2,1,0:T(8,128)S(1)}, f32[1,16,512]{2,1,0:T(8,128)}, u32[]{:S(2)}) copy-start(f32[1,16,512]{2,1,0:T(8,128)} %param.10) | copy-start | bytes 98308
  0.8 0.7 copy-start.1

commit v2 on v1

v2 whole, which is shorter than its diff:
```python
import functools

import jax
import jax.numpy as jnp
from jax import lax
from jax.experimental import pallas as pl
from jax.experimental.pallas import tpu as pltpu
from jax.sharding import PartitionSpec as P

MESH = pl.DeviceIdType.MESH
F32 = jnp.float32
BF16 = jnp.bfloat16
DH = 128
SCHEDULE = (
    "S0 s0 S1 r",
    "I s1 S2 S3",
    "I I I I",
    "W0 s2 T0 I",
    "I W1 s3 T1",
    "G0 I I K0",
    "I G1 I X0",
    "W2 T2 K1 I",
    "I G2 X1 I",
    "W3 T3 K2 I",
    "G3 X2 I K3",
    "O00 O02 O01 O03",
    "X3 O10 O12 O11",
    "O13 O20 O22 O21",
    "O23 O30 O32 O31",
    "O33",
)
PAD = 8
HIGHEST = lax.Precision.HIGHEST


def kernel(
    dims,
    q_hbm, k_hbm, v_hbm, g_hbm, ld_hbm, gain_hbm,
    o,
    q, k, v, g,
    ld, ld_mine, run_ld, gain_in, gain,
    cum_row, dec_row, cum_col, exp_col, run_decay, all_decay,
    s_out, s_in, b_out, b_in, t_out, t_in, c_now, c_out, c_in, p_out, p_in,
    inside, gated,
    load_sem,
    ld_send, ld_recv, other_send, other_recv, gain_send, gain_recv,
    s_send, s_recv, b_send, b_recv, t_send, t_recv, c_send, c_recv, p_send, p_recv,
):
    ny, nx, nz, chunks, few = dims
    rows = q.shape[0]
    per_owner = chunks * few
    heads = 2 * ny * per_owner
    pieces = nz // few
    runs = 2 * ny
    piece = DH // pieces
    y = lax.axis_index("head")
    ctx = lax.axis_index("ctx")
    x = ctx // (2 * nz)
    z = (ctx // 2) % nz
    core = ctx % 2

    def at(x, z, core):
        return {"ctx": (x * nz + z) * 2 + core}

    def load(n, src, dst):
        return pltpu.make_async_copy(src, dst, load_sem.at[n])

    loads = [
        load(0, ld_hbm, ld),
        load(1, gain_hbm, gain_in.at[y]),
        load(2, k_hbm, k),
        load(3, v_hbm, v),
        load(4, q_hbm, q),
        load(5, g_hbm, g),
    ]
    for one in loads:
        one.start()

    barrier = pltpu.get_barrier_semaphore()
    column = [(d, f) for d in (2, 1, 3, 0) for f in (0, 1) if d < ny and (d, f) != (0, 0)]

    def core_at(f):
        return 1 - core if f else core

    def column_peer(d, f):
        return {"head": lax.rem(y + d, ny), **at(x, z, core_at(f))}

    def nth(d, f):
        return 2 * d + f - 1

    peers = [column_peer(d, f) for d, f in column]
    peers += [at(x, lax.rem(z + e, nz), core) for e in range(1, nz)]
    peers += [at(lax.rem(x + d, nx), z, core) for d in range(1, nx)]
    for peer in peers:
        pl.semaphore_signal(barrier, inc=1, device_id=peer, device_id_type=MESH)
    pl.semaphore_wait(barrier, len(peers))

    def remote(src, dst, send, recv, peer):
        return pltpu.make_async_remote_copy(
            src_ref=src, dst_ref=dst, send_sem=send, recv_sem=recv,
            device_id=peer, device_id_type=MESH,
        )

    def ld_copy(d, source, reader):
        theirs = pl.ds(pl.multiple_of(reader * rows, rows), rows)
        return remote(
            ld.at[:, theirs], ld_mine.at[source], ld_send.at[d - 1], ld_recv.at[d - 1],
            {"head": lax.rem(y + d, ny)},
        )

    def gain_copy(d, source):
        peer = {"head": lax.rem(y + d, ny)}
        return remote(
            gain_in.at[source], gain_in.at[source], gain_send.at[d - 1], gain_recv.at[d - 1], peer
        )

    def other_copy(half, block):
        rows_of = pl.ds(pl.multiple_of(half * per_owner, per_owner), per_owner)
        return remote(
            ld.at[rows_of], run_ld.at[block], other_send.at[0], other_recv.at[0], column_peer(0, 1)
        )

    loads[0].wait()
    for d in range(1, ny):
        ld_copy(d, y, lax.rem(y + d, ny)).start()
    mine = pl.ds(pl.multiple_of(y * rows, rows), rows)
    other_copy(1 - core, core).start()
    loads[1].wait()
    for d in range(1, ny):
        gain_copy(d, y).start()
    ld_mine[y] = ld[:, mine]
    run_ld[core] = ld[pl.ds(pl.multiple_of(core * per_owner, per_owner), per_owner), :]
    for d in range(1, ny):
        ld_copy(d, lax.rem(y + ny - d, ny), y).wait_recv()

    upper = (
        lax.broadcasted_iota(jnp.int32, (rows, rows), 0)
        <= lax.broadcasted_iota(jnp.int32, (rows, rows), 1)
    ).astype(F32)
    cum_col[...] = jnp.zeros_like(cum_col)
    for group in range(ny):
        cumulative = jnp.dot(
            ld_mine[group], upper, precision=HIGHEST, preferred_element_type=F32
        )
        here = pl.ds(group * 2 * per_owner, 2 * per_owner)
        cum_row[here, :] = cumulative
        dec_row[here, :] = jnp.exp(cumulative[:, rows - 1 :] - cumulative)
        cum_col[here, :] = cumulative
    cum_col[...] = cum_col[...].T
    exp_col[...] = jnp.exp(cum_col[...])

    def make_decays():
        other_copy(core, 1 - core).wait_recv()
        whole = jnp.zeros((per_owner, 1), F32)
        for run in range(runs):
            part = run_ld[run // ny, :, run % ny * rows : (run % ny + 1) * rows]
            total = jnp.sum(part, axis=1, keepdims=True)
            run_decay[run] = jnp.broadcast_to(jnp.exp(total), (per_owner, DH))
            whole = whole + total
        all_decay[...] = jnp.broadcast_to(jnp.exp(whole), (per_owner, DH))

    def s_copy(i, d, f, source, group, half):
        first = (group * 2 + half) * per_owner + i * few
        there = pl.ds(i * few, few)
        return remote(
            s_out.at[pl.ds(first, few)], s_in.at[source, there],
            s_send.at[i, nth(d, f)], s_recv.at[i, nth(d, f)], column_peer(d, f),
        )

    def s_sent(i, d, f):
        return s_copy(i, d, f, core * ny + y, lax.rem(y + d, ny), core_at(f))

    def s_got(i, d, f):
        return s_copy(i, d, f, core_at(f) * ny + lax.rem(y + ny - d, ny), y, core)

    def b_copy(i, e, source, owner):
        return remote(
            b_out.at[i, owner], b_in.at[i, source], b_send.at[i, e - 1], b_recv.at[i, e - 1],
            at(x, owner, core),
        )

    def t_copy(i, d):
        return remote(
            t_out.at[i], t_in.at[i, d - 1], t_send.at[i, d - 1], t_recv.at[i, d - 1],
            at(lax.rem(x + d, nx), z, core),
        )

    def c_copy(i, e, source, chip):
        return remote(
            c_out.at[i, chip], c_in.at[i, source], c_send.at[i, e - 1], c_recv.at[i, e - 1],
            at(x, chip, core),
        )

    def p_copy(i, d, f, run, group, half):
        there = pl.ds(i * few, few)
        return remote(
            p_out.at[run, there], p_in.at[group * 2 + half, there],
            p_send.at[i, nth(d, f)], p_recv.at[i, nth(d, f)], column_peer(d, f),
        )

    def p_sent(i, d, f):
        return p_copy(i, d, f, core_at(f) * ny + lax.rem(y + d, ny), y, core)

    def p_got(i, d, f):
        return p_copy(i, d, f, core * ny + y, lax.rem(y + ny - d, ny), core_at(f))

    def lanes_of(first, j):
        return pl.ds(pl.multiple_of((first + j) * DH, DH), DH)

    z_order = [e for e in (2, 1, 3) if e < nz]

    def make_states(i):
        for d, f in column + [(0, 0)]:
            begin = pl.multiple_of(
                (lax.rem(y + d, ny) * 2 + core_at(f)) * per_owner, per_owner
            )
            decays = dec_row[pl.ds(begin, per_owner), :]
            for j in range(i * few, (i + 1) * few):
                lanes = lanes_of(begin, j)
                decayed = (k[:, lanes].T.astype(F32) * decays[j : j + 1]).astype(BF16)
                state = jnp.dot(decayed, v[:, lanes], preferred_element_type=F32).astype(BF16)
                if (d, f) == (0, 0):
                    s_in[core * ny + y, j] = state
                else:
                    s_out[begin + j] = state

    def send_states(i):
        for d, f in column:
            s_sent(i, d, f).start()

    causal = lax.broadcasted_iota(jnp.int32, (rows, rows), 0) >= lax.broadcasted_iota(
        jnp.int32, (rows, rows), 1
    )
    def make_inside(first, count):
        for head in range(first, first + count):
            lanes = slice(head * DH, (head + 1) * DH)
            scores = lax.dot_general(
                q[:, lanes], k[:, lanes], (((1,), (1,)), ((), ())), preferred_element_type=F32
            )
            gap = cum_col[:, head : head + 1] - cum_row[head : head + 1, :]
            weights = (scores * jnp.exp(jnp.where(causal, gap, -jnp.inf))).astype(BF16)
            inside[:, lanes] = jnp.dot(weights, v[:, lanes], preferred_element_type=F32)
            gated[:, lanes] = jax.nn.sigmoid(g[:, lanes].astype(F32)) * gain[head : head + 1, :]

    def await_states(i):
        for d, f in column:
            s_got(i, d, f).wait_recv()

    def make_totals(i):
        for j in range(few):
            local = i * few + j
            total = s_in[0, local].astype(F32)
            for run in range(1, runs):
                total = total * run_decay[run, local : local + 1, :] + s_in[run, local].astype(F32)
            for n in range(pieces):
                b_out[i, j * pieces + n, :piece, :] = total[n * piece : (n + 1) * piece]
                b_out[i, j * pieces + n, piece:, :] = jnp.broadcast_to(
                    all_decay[local : local + 1, :], (PAD, DH)
                )
        for e in z_order:
            b_copy(i, e, z, lax.rem(z + e, nz)).start()
        b_in[i, z] = b_out[i, z]

    def make_group_total(i):
        for e in range(1, nz):
            b_copy(i, e, lax.rem(z + nz - e, nz), lax.rem(z + e, nz)).wait_recv()
        total = b_in[i, 0, :piece, :]
        decay = b_in[i, 0, piece:, :]
        for chip in range(1, nz):
            step = b_in[i, chip, piece:, :]
            total = total * step[:1] + b_in[i, chip, :piece, :]
            decay = decay * step
        t_out[i, :piece, :] = total
        t_out[i, piece:, :] = decay
        for d in range(1, nx):

            @pl.when(x + d < nx)
            def _(d=d):
                t_copy(i, d).start()

    def make_carried(i):
        c_now[...] = jnp.zeros_like(c_now)
        for d in range(nx - 1, 0, -1):

            @pl.when(x >= d)
            def _(d=d):
                t_copy(i, d).wait_recv()
                c_now[...] = c_now[...] * t_in[i, d - 1, piece : piece + 1, :] + t_in[i, d - 1, :piece, :]

        state = c_now[...]
        for chip in range(nz):
            c_out[i, chip] = state
            if chip + 1 < nz:
                state = state * b_in[i, chip, piece : piece + 1, :] + b_in[i, chip, :piece, :]
        for e in z_order:
            c_copy(i, e, z, lax.rem(z + e, nz)).start()
        c_in[i, z] = c_out[i, z]

    def make_prefixes(i):
        for e in range(1, nz):
            c_copy(i, e, lax.rem(z + nz - e, nz), lax.rem(z + e, nz)).wait_recv()
        for j in range(few):
            local = i * few + j
            state = c_in[i, j * pieces : (j + 1) * pieces].reshape(DH, DH)
            for run in range(runs):
                p_out[run, local] = state.astype(BF16)
                if run + 1 < runs:
                    decay = run_decay[run, local : local + 1, :]
                    state = state * decay + s_in[run, local].astype(F32)
        for d, f in column:
            p_sent(i, d, f).start()
        there = pl.ds(i * few, few)
        p_in[y * 2 + core, there] = p_out[core * ny + y, there]

    def make_outputs(i, d):
        group = lax.rem(y + ny - d, ny)
        for f in (0, 1):
            if (d, f) in column:
                p_got(i, d, f).wait_recv()
        for half in (0, 1):
            first = (group * 2 + half) * per_owner + i * few
            columns = pltpu.roll(exp_col[...], lax.rem(DH - first, DH), axis=1)[:, :few]
            for j in range(few):
                lanes = lanes_of(first, j)
                from_state = jnp.dot(
                    q[:, lanes], p_in[group * 2 + half, i * few + j], preferred_element_type=F32
                )
                mixed = inside[:, lanes] + columns[:, j : j + 1] * from_state
                scale = lax.rsqrt(jnp.mean(mixed * mixed, axis=1, keepdims=True) + 1e-6)
                o[:, lanes] = (mixed * scale * gated[:, lanes]).astype(BF16)

    def ready_rest():
        loads[4].wait()
        loads[5].wait()
        for d in range(1, ny):
            gain_copy(d, lax.rem(y + ny - d, ny)).wait_recv()
        for group in range(ny):
            gain[pl.ds(group * 2 * per_owner, 2 * per_owner), :] = gain_in[group].astype(F32)
        make_decays()

    sixteenth = heads // 16
    loads[2].wait()
    loads[3].wait()
    plan = " ".join(SCHEDULE).split()
    inner = iter(range(16))
    calls = dict(
        S=make_states, s=send_states, W=await_states, T=make_totals,
        G=make_group_total, K=make_carried, X=make_prefixes,
    )
    for word in plan:
        if word == "r":
            ready_rest()
        elif word == "I":
            make_inside(next(inner) * sixteenth, sixteenth)
        elif word[0] == "O":
            make_outputs(int(word[1]), int(word[2]))
        else:
            calls[word[0]](int(word[1]))

    for d in range(1, ny):
        ld_copy(d, y, lax.rem(y + d, ny)).wait_send()
        gain_copy(d, y).wait_send()
    other_copy(1 - core, core).wait_send()
    for i in range(chunks):
        for d, f in column:
            s_sent(i, d, f).wait_send()
            p_sent(i, d, f).wait_send()
        for e in range(1, nz):
            b_copy(i, e, z, lax.rem(z + e, nz)).wait_send()
            c_copy(i, e, z, lax.rem(z + e, nz)).wait_send()
        for d in range(1, nx):

            @pl.when(x + d < nx)
            def _(i=i, d=d):
                t_copy(i, d).wait_send()


def on_device(dims, queries, keys, values, gate, log_decay, norm_gain):
    ny, nx, nz, chunks, few = dims
    per_owner = chunks * few
    piece = DH * few // nz
    runs = 2 * ny
    heads = runs * per_owner
    _, rows, width = queries.shape
    block = log_decay.shape[2]
    dma = pltpu.SemaphoreType.DMA
    vmem = pltpu.VMEM
    stream = [vmem((rows, width), BF16)] * 4
    out = pl.pallas_call(
        functools.partial(kernel, dims),
        out_shape=pltpu.VMEM((rows, width), BF16),
        in_specs=[pl.BlockSpec(memory_space=pltpu.HBM)] * 6,
        out_specs=pl.BlockSpec(memory_space=pltpu.VMEM),
        scratch_shapes=stream
        + [
            vmem((2 * per_owner, block), F32),
            vmem((ny, 2 * per_owner, rows), F32),
            vmem((2, per_owner, block), F32),
            vmem((ny, 2 * per_owner, DH), BF16),
            vmem((heads, DH), F32),
            vmem((heads, rows), F32),
            vmem((heads, rows), F32),
            vmem((rows, rows), F32),
            vmem((rows, rows), F32),
            vmem((runs, per_owner, DH), F32),
            vmem((per_owner, DH), F32),
            vmem((heads, DH, DH), BF16),
            vmem((runs, per_owner, DH, DH), BF16),
            vmem((chunks, nz, piece + PAD, DH), F32),
            vmem((chunks, nz, piece + PAD, DH), F32),
            vmem((chunks, piece + PAD, DH), F32),
            vmem((chunks, nx - 1, piece + PAD, DH), F32),
            vmem((piece, DH), F32),
            vmem((chunks, nz, piece, DH), F32),
            vmem((chunks, nz, piece, DH), F32),
            vmem((runs, per_owner, DH, DH), BF16),
            vmem((runs, per_owner, DH, DH), BF16),
            vmem((rows, width), F32),
            vmem((rows, width), F32),
            dma((6,)),
            dma((ny - 1,)),
            dma((ny - 1,)),
            dma((1,)),
            dma((1,)),
            dma((ny - 1,)),
            dma((ny - 1,)),
            dma((chunks, runs - 1)),
            dma((chunks, runs - 1)),
            dma((chunks, nz - 1)),
            dma((chunks, nz - 1)),
            dma((chunks, nx - 1)),
            dma((chunks, nx - 1)),
            dma((chunks, nz - 1)),
            dma((chunks, nz - 1)),
            dma((chunks, runs - 1)),
            dma((chunks, runs - 1)),
        ],
        compiler_params=pltpu.CompilerParams(
            collective_id=0, has_side_effects=True, vmem_limit_bytes=52 * 2**20
        ),
        cost_estimate=pl.CostEstimate(
            flops=8 * rows * DH * width, bytes_accessed=10 * rows * width, transcendentals=0
        ),
    )(
        queries[0],
        keys[0],
        values[0],
        gate[0],
        log_decay[0],
        norm_gain.reshape(2 * per_owner, DH),
    )
    return out[None]


def solution(mesh):
    ny = mesh.shape["head"]
    nctx = mesh.shape["ctx"]
    nx = 4 if nctx >= 16 else 2
    def whole(queries, keys, values, gate, log_decay, norm_gain):
        chunks = 4
        few = log_decay.shape[1] // (2 * ny * chunks)
        dims = (ny, nx, nctx // (2 * nx), chunks, few)
        return jax.shard_map(
            functools.partial(on_device, dims),
            mesh=mesh,
            in_specs=(P("ctx", "head", None),) * 5 + (P("head"),),
            out_specs=P("ctx", "head", None),
            check_vma=False,
        )(queries, keys, values, gate, log_decay, norm_gain)

    return whole
```

time: 75 us -> 60.6 us (0.81)
  Pallas kernels: 70 us -> 59.2 us
  local copies, waits for them, and re-layouts: 4.54 us -> 1.32 us
    pallas_call x1, Pallas kernels: 70 us -> 59.2 us  [on_device(): pl.pallas_call(functools.partial(kernel, dims), out_shape=pltpu.VMEM((row...]
    unnamed x5 -> x1, local copies, waits for them, and re-layouts: 4.54 us -> 1.32 us
where the time goes in v2:
time: 60.6 us; the launch traced here: 60.5 us
  Pallas kernels  59.2 us (98%)
  local copies, waits for them, and re-layouts  1.32 us (2%)
    pallas_call x1, Pallas kernels, on_device(): pl.pallas_call(functools.partial(kernel, dims), out_shape=pltpu.VMEM((row...  59.2 us
    unnamed x1, local copies, waits for them, and re-layouts  1.32 us

profile of v2, /device:TPU:7, one launch (start us, length us, event | category | flops | bytes accessed | tf_op | source)
XLA Modules:
  0.0 60.5 jit_solution(11100423446884191025)
XLA Ops:
  0.0 59.2 %shard_map.64 = bf16[128,8192]{1,0:T(8,128)(2,1)S(1)} custom-call(bf16[128,8192]{1,0:T(8,128)(2,1)} %bitcast.8, bf16[128,8192]{1,0:T(8,128)(2,1)} %bitcast.9, bf16[128,8192]{1,0:T(8,128)(2,1)} %bitcast.10, bf16[128,8192]{1,0:T(8,128)(2,1)} %bitcast.11, f32[16,512]{1,0:T(8,128)} %bitcast.12, bf16[16,128]{1,0:T(8,128)(2,1)} %bitcast.13), custom_call_target="tpu_custom_call" | custom-call | flops 1073741824 | bytes 10485760 | tf_op jit(solution)/shard_map/pallas_call | solution.py:389
  59.2 1.3 %copy.8 = bf16[1,128,8192]{2,1,0:T(8,128)(2,1)} copy(bf16[1,128,8192]{2,1,0:T(8,128)(2,1)S(1)} %bitcast.7) | data formatting | bytes 4194304

commit v3 on v2

--- a/solution.py
+++ b/solution.py
@@ -11,10 +11,11 @@
 F32 = jnp.float32
 BF16 = jnp.bfloat16
 DH = 128
+CHUNKS = 4
 SCHEDULE = (
-    "S0 s0 S1 r",
-    "I s1 S2 S3",
-    "I I I I",
+    "F0 S1 r I",
+    "s1 S2 S3 I",
+    "I I I A0",
     "W0 s2 T0 I",
     "I W1 s3 T1",
     "G0 I I K0",
@@ -23,11 +24,14 @@
     "I G2 X1 I",
     "W3 T3 K2 I",
     "G3 X2 I K3",
-    "O00 O02 O01 O03",
-    "X3 O10 O12 O11",
-    "O13 O20 O22 O21",
-    "O23 O30 O32 O31",
-    "O33",
+    "U0 U1 O00 O02",
+    "O01 O03 X3 U2",
+    "M0 M1 O10 O12",
+    "O11 O13 P0 U3",
+    "M2 M3 O20 O22",
+    "O21 O23 P1 P2",
+    "O30 O32 O31 O33",
+    "P3",
 )
 PAD = 8
 HIGHEST = lax.Precision.HIGHEST
@@ -137,7 +141,6 @@
         lax.broadcasted_iota(jnp.int32, (rows, rows), 0)
         <= lax.broadcasted_iota(jnp.int32, (rows, rows), 1)
     ).astype(F32)
-    cum_col[...] = jnp.zeros_like(cum_col)
     for group in range(ny):
         cumulative = jnp.dot(
             ld_mine[group], upper, precision=HIGHEST, preferred_element_type=F32
@@ -145,9 +148,13 @@
         here = pl.ds(group * 2 * per_owner, 2 * per_owner)
         cum_row[here, :] = cumulative
         dec_row[here, :] = jnp.exp(cumulative[:, rows - 1 :] - cumulative)
-        cum_col[here, :] = cumulative
-    cum_col[...] = cum_col[...].T
-    exp_col[...] = jnp.exp(cum_col[...])
+
+    def make_columns():
+        cum_col[:heads, :] = cum_row[...]
+        if heads < rows:
+            cum_col[heads:, :] = jnp.zeros((rows - heads, rows), F32)
+        cum_col[...] = cum_col[...].T
+        exp_col[...] = jnp.exp(cum_col[...])
 
     def make_decays():
         other_copy(core, 1 - core).wait_recv()
@@ -209,7 +216,7 @@
 
     z_order = [e for e in (2, 1, 3) if e < nz]
 
-    def make_states(i):
+    def make_states(i, send=False):
         for d, f in column + [(0, 0)]:
             begin = pl.multiple_of(
                 (lax.rem(y + d, ny) * 2 + core_at(f)) * per_owner, per_owner
@@ -223,6 +230,8 @@
                     s_in[core * ny + y, j] = state
                 else:
                     s_out[begin + j] = state
+            if send and (d, f) != (0, 0):
+                s_sent(i, d, f).start()
 
     def send_states(i):
         for d, f in column:
@@ -336,7 +345,33 @@
             gain_copy(d, lax.rem(y + ny - d, ny)).wait_recv()
         for group in range(ny):
             gain[pl.ds(group * 2 * per_owner, 2 * per_owner), :] = gain_in[group].astype(F32)
+        make_columns()
         make_decays()
+
+    def drain_first(_):
+        for d in range(1, ny):
+            ld_copy(d, y, lax.rem(y + d, ny)).wait_send()
+            gain_copy(d, y).wait_send()
+        other_copy(1 - core, core).wait_send()
+
+    def drain_up(i):
+        for d, f in column:
+            s_sent(i, d, f).wait_send()
+        for e in range(1, nz):
+            b_copy(i, e, z, lax.rem(z + e, nz)).wait_send()
+
+    def drain_middle(i):
+        for e in range(1, nz):
+            c_copy(i, e, z, lax.rem(z + e, nz)).wait_send()
+        for d in range(1, nx):
+
+            @pl.when(x + d < nx)
+            def _(d=d):
+                t_copy(i, d).wait_send()
+
+    def drain_down(i):
+        for d, f in column:
+            p_sent(i, d, f).wait_send()
 
     sixteenth = heads // 16
     loads[2].wait()
@@ -344,8 +379,9 @@
     plan = " ".join(SCHEDULE).split()
     inner = iter(range(16))
     calls = dict(
-        S=make_states, s=send_states, W=await_states, T=make_totals,
+        S=make_states, s=send_states, F=functools.partial(make_states, send=True), W=await_states, T=make_totals,
         G=make_group_total, K=make_carried, X=make_prefixes,
+        A=drain_first, U=drain_up, M=drain_middle, P=drain_down,
     )
     for word in plan:
         if word == "r":
@@ -356,23 +392,6 @@
             make_outputs(int(word[1]), int(word[2]))
         else:
             calls[word[0]](int(word[1]))
-
-    for d in range(1, ny):
-        ld_copy(d, y, lax.rem(y + d, ny)).wait_send()
-        gain_copy(d, y).wait_send()
-    other_copy(1 - core, core).wait_send()
-    for i in range(chunks):
-        for d, f in column:
-            s_sent(i, d, f).wait_send()
-            p_sent(i, d, f).wait_send()
-        for e in range(1, nz):
-            b_copy(i, e, z, lax.rem(z + e, nz)).wait_send()
-            c_copy(i, e, z, lax.rem(z + e, nz)).wait_send()
-        for d in range(1, nx):
-
-            @pl.when(x + d < nx)
-            def _(i=i, d=d):
-                t_copy(i, d).wait_send()
 
 
 def on_device(dims, queries, keys, values, gate, log_decay, norm_gain):
@@ -457,7 +476,7 @@
     nctx = mesh.shape["ctx"]
     nx = 4 if nctx >= 16 else 2
     def whole(queries, keys, values, gate, log_decay, norm_gain):
-        chunks = 4
+        chunks = CHUNKS
         few = log_decay.shape[1] // (2 * ny * chunks)
         dims = (ny, nx, nctx // (2 * nx), chunks, few)
         return jax.shard_map(

time: 60.6 us -> 60.3 us (level)
  no operation moved by 1% of the time
where the time goes in v3:
time: 60.3 us; the launch traced here: 60.1 us
  Pallas kernels  58.8 us (98%)
  local copies, waits for them, and re-layouts  1.32 us (2%)
    pallas_call x1, Pallas kernels, on_device(): pl.pallas_call(functools.partial(kernel, dims), out_shape=pltpu.VMEM((row...  58.8 us
    unnamed x1, local copies, waits for them, and re-layouts  1.32 us

profile of v3, /device:TPU:7, one launch (start us, length us, event | category | flops | bytes accessed | tf_op | source)
XLA Modules:
  0.0 60.1 jit_solution(17500976546599178872)
XLA Ops:
  0.0 58.8 %shard_map.64 = bf16[128,8192]{1,0:T(8,128)(2,1)S(1)} custom-call(bf16[128,8192]{1,0:T(8,128)(2,1)} %bitcast.8, bf16[128,8192]{1,0:T(8,128)(2,1)} %bitcast.9, bf16[128,8192]{1,0:T(8,128)(2,1)} %bitcast.10, bf16[128,8192]{1,0:T(8,128)(2,1)} %bitcast.11, f32[16,512]{1,0:T(8,128)} %bitcast.12, bf16[16,128]{1,0:T(8,128)(2,1)} %bitcast.13), custom_call_target="tpu_custom_call" | custom-call | flops 1073741824 | bytes 10485760 | tf_op jit(solution)/shard_map/pallas_call | solution.py:408
  58.8 1.3 %copy.8 = bf16[1,128,8192]{2,1,0:T(8,128)(2,1)} copy(bf16[1,128,8192]{2,1,0:T(8,128)(2,1)S(1)} %bitcast.7) | data formatting | bytes 4194304

commit v4 on v3

--- a/solution.py
+++ b/solution.py
@@ -125,7 +125,7 @@
         )
 
     loads[0].wait()
-    for d in range(1, ny):
+    for d in [d for d in (2, 1, 3) if d < ny]:
         ld_copy(d, y, lax.rem(y + d, ny)).start()
     mine = pl.ds(pl.multiple_of(y * rows, rows), rows)
     other_copy(1 - core, core).start()
@@ -134,20 +134,20 @@
         gain_copy(d, y).start()
     ld_mine[y] = ld[:, mine]
     run_ld[core] = ld[pl.ds(pl.multiple_of(core * per_owner, per_owner), per_owner), :]
-    for d in range(1, ny):
-        ld_copy(d, lax.rem(y + ny - d, ny), y).wait_recv()
-
     upper = (
         lax.broadcasted_iota(jnp.int32, (rows, rows), 0)
         <= lax.broadcasted_iota(jnp.int32, (rows, rows), 1)
     ).astype(F32)
-    for group in range(ny):
-        cumulative = jnp.dot(
-            ld_mine[group], upper, precision=HIGHEST, preferred_element_type=F32
-        )
-        here = pl.ds(group * 2 * per_owner, 2 * per_owner)
-        cum_row[here, :] = cumulative
-        dec_row[here, :] = jnp.exp(cumulative[:, rows - 1 :] - cumulative)
+    loads[2].wait()
+    loads[3].wait()
+    for d in range(1, ny):
+        ld_copy(d, lax.rem(y + ny - d, ny), y).wait_recv()
+
+    cumulative = jnp.dot(
+        ld_mine[...].reshape(heads, rows), upper, precision=HIGHEST, preferred_element_type=F32
+    )
+    dec_row[...] = jnp.exp(cumulative[:, rows - 1 :] - cumulative)
+    cum_row[...] = cumulative
 
     def make_columns():
         cum_col[:heads, :] = cum_row[...]
@@ -374,8 +374,6 @@
             p_sent(i, d, f).wait_send()
 
     sixteenth = heads // 16
-    loads[2].wait()
-    loads[3].wait()
     plan = " ".join(SCHEDULE).split()
     inner = iter(range(16))
     calls = dict(

time: 60.3 us -> 60.2 us (level)
  no operation moved by 1% of the time
where the time goes in v4:
time: 60.2 us; the launch traced here: 60 us
  Pallas kernels  58.7 us (98%)
  local copies, waits for them, and re-layouts  1.32 us (2%)
    pallas_call x1, Pallas kernels, on_device(): pl.pallas_call(functools.partial(kernel, dims), out_shape=pltpu.VMEM((row...  58.7 us
    unnamed x1, local copies, waits for them, and re-layouts  1.32 us

profile of v4, /device:TPU:7, one launch (start us, length us, event | category | flops | bytes accessed | tf_op | source)
XLA Modules:
  0.0 60.0 jit_solution(9963101479405140056)
XLA Ops:
  0.0 58.7 %shard_map.64 = bf16[128,8192]{1,0:T(8,128)(2,1)S(1)} custom-call(bf16[128,8192]{1,0:T(8,128)(2,1)} %bitcast.8, bf16[128,8192]{1,0:T(8,128)(2,1)} %bitcast.9, bf16[128,8192]{1,0:T(8,128)(2,1)} %bitcast.10, bf16[128,8192]{1,0:T(8,128)(2,1)} %bitcast.11, f32[16,512]{1,0:T(8,128)} %bitcast.12, bf16[16,128]{1,0:T(8,128)(2,1)} %bitcast.13), custom_call_target="tpu_custom_call" | custom-call | flops 1073741824 | bytes 10485760 | tf_op jit(solution)/shard_map/pallas_call | solution.py:406
  58.7 1.3 %copy.8 = bf16[1,128,8192]{2,1,0:T(8,128)(2,1)} copy(bf16[1,128,8192]{2,1,0:T(8,128)(2,1)S(1)} %bitcast.7) | data formatting | bytes 4194304

commit v5 on v4

--- a/solution.py
+++ b/solution.py
@@ -94,10 +94,17 @@
 
     peers = [column_peer(d, f) for d, f in column]
     peers += [at(x, lax.rem(z + e, nz), core) for e in range(1, nz)]
-    peers += [at(lax.rem(x + d, nx), z, core) for d in range(1, nx)]
     for peer in peers:
         pl.semaphore_signal(barrier, inc=1, device_id=peer, device_id_type=MESH)
-    pl.semaphore_wait(barrier, len(peers))
+    for d in range(1, nx):
+
+        @pl.when(x >= d)
+        def _(d=d):
+            pl.semaphore_signal(
+                barrier, inc=1, device_id=at(x - d, z, core), device_id_type=MESH
+            )
+
+    pl.semaphore_wait(barrier, len(peers) + nx - 1 - x)
 
     def remote(src, dst, send, recv, peer):
         return pltpu.make_async_remote_copy(

time: 60.2 us -> 60.3 us (level)
  no operation moved by 1% of the time
where the time goes in v5:
time: 60.3 us; the launch traced here: 60 us
  Pallas kernels  58.7 us (97%)
  local copies, waits for them, and re-layouts  1.32 us (2%)
    pallas_call x1, Pallas kernels, on_device(): pl.pallas_call(functools.partial(kernel, dims), out_shape=pltpu.VMEM((row...  58.7 us
    unnamed x1, local copies, waits for them, and re-layouts  1.32 us

profile of v5, /device:TPU:7, one launch (start us, length us, event | category | flops | bytes accessed | tf_op | source)
XLA Modules:
  0.0 60.0 jit_solution(822540116793383385)
XLA Ops:
  0.0 58.7 %shard_map.64 = bf16[128,8192]{1,0:T(8,128)(2,1)S(1)} custom-call(bf16[128,8192]{1,0:T(8,128)(2,1)} %bitcast.8, bf16[128,8192]{1,0:T(8,128)(2,1)} %bitcast.9, bf16[128,8192]{1,0:T(8,128)(2,1)} %bitcast.10, bf16[128,8192]{1,0:T(8,128)(2,1)} %bitcast.11, f32[16,512]{1,0:T(8,128)} %bitcast.12, bf16[16,128]{1,0:T(8,128)(2,1)} %bitcast.13), custom_call_target="tpu_custom_call" | custom-call | flops 1073741824 | bytes 10485760 | tf_op jit(solution)/shard_map/pallas_call | solution.py:413
  58.7 1.3 %copy.8 = bf16[1,128,8192]{2,1,0:T(8,128)(2,1)} copy(bf16[1,128,8192]{2,1,0:T(8,128)(2,1)S(1)} %bitcast.7) | data formatting | bytes 4194304
